TPU v7x, 32 devices: a whole 2x2x4 slice. The times are simulated.
32 devices in a mesh: tok: 8 (over z, y), head: 4 (over x, core).
Axes of the slice: x: 2, y: 2, z: 4, core: 2. Of those that a mesh axis runs over, the one named last changes fastest.
Arguments:
- latents: float32 [512, 4096], P(None, 'tok'), may hold values from -6 to 6
- doc_keys: bfloat16 [2048, 4096], P('tok', 'head'), may hold values from -500 to 500
- doc_values: bfloat16 [2048, 4096], P('tok', 'head'), may hold values from -6 to 6
- token_mask: int32 [2048], P('tok'), may hold values from 0 to 1, as said below
- shard_lengths: int32 [8], P('tok'), may hold values from 64 to 256, as said below
- query_weight: bfloat16 [4096, 4096], P('tok', 'head'), may hold values from -0.375 to 0.375
- output_weight: bfloat16 [4096, 4096], P('head', 'tok'), may hold values from -0.375 to 0.375
- attn_gain: float32 [4096], P('tok'), may hold values from 0.1 to 1.9
- up_weight: bfloat16 [4096, 4096], P('tok', 'head'), may hold values from -0.1875 to 0.1875
- down_weight: bfloat16 [4096, 4096], P('head', 'tok'), may hold values from -0.1875 to 0.1875
- mlp_gain: float32 [4096], P('tok'), may hold values from 0.1 to 1.9
Outputs:
- encoded: float32 [512, 4096], P(None, 'tok')
Inputs may be any that keep to these rules, and one draw needn't show every extreme that they name: `token_mask`: the first token of every aligned block of 256 tokens is 1. Entry j bounds the valid tokens of block j to its first shard_lengths[j]; some entry equals 256.
All inputs are finite; a program needn't handle non-finite values.
Results may differ from a plain program's by a relative error of at most 0.0035.
The roundings to bfloat16 on the way count: a program that leaves them out, or rounds other values in their place, can miss the bound.
Values may be sent and summed in bfloat16 or wider, within the bound.
A program may use at most 64 MiB of HBM per device.

v0:
```python
import jax
import jax.numpy as jnp
from jax import lax
from jax.sharding import PartitionSpec as P

D = 4096
HS = 128


epsilon = 1e-05
masked_score = -1e30


def round_rows(rows):
    return rows.astype(jnp.bfloat16)


def gelu_rows(rows):
    return jax.nn.gelu(rows).astype(jnp.bfloat16)


def projected(state, gain, weight, finish):
    scaled = (state * gain).astype(jnp.bfloat16)
    squares = jnp.sum(state * state, axis=1)
    partial_rows = jnp.dot(scaled, weight, preferred_element_type=jnp.float32)
    squares, summed = lax.psum((squares, partial_rows), "tok")
    inverse = lax.rsqrt(squares / D + epsilon)
    return finish(summed * inverse[:, None])


def head_update(full_rows, weight):
    return lax.psum(jnp.dot(full_rows, weight, preferred_element_type=jnp.float32), "head")


def attend(queries, doc_keys, doc_values, valid):
    heads = doc_keys.shape[1] // HS
    latent_count = queries.shape[0]
    token_count = doc_keys.shape[0]
    query_heads = queries.reshape(latent_count, heads, HS).transpose(1, 0, 2)
    key_heads = doc_keys.reshape(token_count, heads, HS).transpose(1, 0, 2)
    value_heads = doc_values.reshape(token_count, heads, HS).transpose(1, 0, 2)

    def one_head(items):
        query_one, key_one, value_one = items
        scores = lax.dot_general(
            query_one, key_one, (((1,), (1,)), ((), ())), preferred_element_type=jnp.float32
        ) * HS ** (-0.5)
        scores = jnp.where(valid[None, :], scores, masked_score)
        highest = jnp.max(scores, axis=1)
        weights = jnp.exp(scores - highest[:, None])
        total = jnp.sum(weights, axis=1)
        weighted = jnp.dot(
            weights.astype(jnp.bfloat16), value_one, preferred_element_type=jnp.float32
        )
        return (highest, total, weighted)

    highest, total, weighted = lax.map(one_head, (query_heads, key_heads, value_heads))
    return (highest.T, total.T, weighted.transpose(1, 0, 2))


def shards(
    latents,
    doc_keys,
    doc_values,
    token_mask,
    shard_lengths,
    query_weight,
    output_weight,
    attn_gain,
    up_weight,
    down_weight,
    mlp_gain,
):
    positions = jnp.arange(doc_keys.shape[0], dtype=jnp.int32)
    valid = (token_mask == 1) & (positions < shard_lengths[0])
    state = latents
    queries = projected(state, attn_gain, query_weight, round_rows)
    highest, total, weighted = attend(queries, doc_keys, doc_values, valid)
    ceiling = lax.pmax(highest, "tok")
    factor = jnp.exp(highest - ceiling)
    weighted, total = (
        lax.psum_scatter(weighted * factor[:, :, None], "tok", scatter_dimension=0, tiled=True),
        lax.psum_scatter(total * factor, "tok", scatter_dimension=0, tiled=True),
    )
    attended_rows = (
        (weighted / total[:, :, None]).astype(jnp.bfloat16).reshape(weighted.shape[0], -1)
    )
    attended = lax.all_gather(attended_rows, "tok", axis=0, tiled=True)
    state = state + head_update(attended, output_weight)
    hidden = projected(state, mlp_gain, up_weight, gelu_rows)
    return state + head_update(hidden, down_weight)


def solution(mesh):
    in_specs = (
        P(None, "tok"),
        P("tok", "head"),
        P("tok", "head"),
        P("tok"),
        P("tok"),
        P("tok", "head"),
        P("head", "tok"),
        P("tok"),
        P("tok", "head"),
        P("head", "tok"),
        P("tok"),
    )
    out_specs = P(None, "tok")
    return jax.shard_map(shards, mesh=mesh, in_specs=in_specs, out_specs=out_specs, check_vma=False)
```

profile of v0, /device:TPU:0, one launch (start us, length us, event | category | flops | bytes accessed | tf_op | source)
XLA Modules:
  0.0 545.3 jit_solution(3886430689480434885)
XLA Ops:
  6.5 1.2 copy-done
  7.8 3.3 fusion.25
  11.2 0.9 copy-done.2
  12.1 1.0 copy.21
  13.1 1.0 copy.20
  14.8 0.1 multiply_reduce_fusion.1
  14.9 24.1 %psum.43 = f32[512]{0:T(512)S(1)} all-reduce(f32[512]{0:T(512)S(1)} %multiply_reduce_fusion.1), channel_id=1, replica_groups=mesh['tok'=8,'head'=4] {'tok'}, use_global_device_ids=true, to_apply=%region_2.0 | all-reduce | flops 512 | bytes 4096 | tf_op jit(solution)/shard_map/psum | solution.py:26
  39.0 77.0 %all-reduce.5.cloned.1.call-done = f32[512,1024]{1,0:T(8,128)} async-done(((f32[512,1024]{1,0:T(8,128)}), f32[512,1024]{1,0:T(8,128)}) %all-reduce.5.cloned.1.call-update) | async-done | bytes 2097168 | tf_op jit(solution)/shard_map/psum | solution.py:26
  116.1 1.8 bitcast_bitcast_fusion
  117.9 25.8 %while.14 = (s32[]{:T(128)}, f32[8,512]{1,0:T(8,128)S(1)}, f32[8,512]{1,0:T(8,128)S(1)}, f32[8,512,128]{2,1,0:T(8,128)}, pred[256]{0:T(512)(128)(4,1)S(1)}, /*in...) while((s32[]{:T(128)}, f32[8,512]{1,0:T(8,128)S(1)}, ...), condition=%wide.region_6.7_spmd, body=%wide.region_3.6_spmd.sunk | while | flops 68025344 | bytes 2116205 | solution.py:57
  117.9 1.1 fusion.50
  119.0 1.8 fusion.52
  120.9 0.1 fusion.51
  121.0 0.1 dynamic_update_slice.17
  121.0 0.1 dynamic_update_slice.16
  121.1 1.1 fusion.50
  122.2 1.8 fusion.52
  124.1 0.1 fusion.51
  124.2 0.1 dynamic_update_slice.17
  124.2 0.1 dynamic_update_slice.16
  124.3 1.1 fusion.50
  125.4 1.8 fusion.52
  127.3 0.1 fusion.51
  127.4 0.1 dynamic_update_slice.17
  127.4 0.1 dynamic_update_slice.16
  127.5 1.1 fusion.50
  128.7 1.8 fusion.52
  130.5 0.1 fusion.51
  130.6 0.1 dynamic_update_slice.17
  130.7 0.1 dynamic_update_slice.16
  130.8 1.1 fusion.50
  131.9 1.9 fusion.52
  133.7 0.1 fusion.51
  133.9 0.1 dynamic_update_slice.16
  134.0 1.1 fusion.50
  135.1 1.9 fusion.52
  137.0 0.1 fusion.51
  137.1 0.1 dynamic_update_slice.17
  137.1 0.1 dynamic_update_slice.16
  137.2 1.1 fusion.50
  138.3 1.8 fusion.52
  140.2 0.1 fusion.51
  140.3 0.1 dynamic_update_slice.16
  140.4 1.1 fusion.50
  141.6 1.8 fusion.52
  143.4 0.1 fusion.51
  143.6 0.1 dynamic_update_slice.16
  143.6 35.8 %pmax.7 = f32[512,8]{0,1:T(8,128)S(1)} all-reduce(f32[512,8]{0,1:T(8,128)S(1)} %bitcast.70), channel_id=1, replica_groups=mesh['tok'=8,'head'=4] {'tok'}, use_global_device_ids=true, to_apply=%region_7.8 | all-reduce | flops 4096 | bytes 32768 | tf_op jit(solution)/shard_map/pmax | solution.py:79
  179.4 0.8 copy.25
  180.4 3.5 bitcast_multiply_fusion
  183.9 55.4 %reduce-scatter.7.cloned.1.call-done = f32[64,8]{1,0:T(8,128)} async-done(((f32[512,8]{1,0:T(8,128)}), f32[64,8]{1,0:T(8,128)}) %reduce-scatter.7.cloned.1.call-update) | async-done | bytes 2064
  239.3 0.8 copy.26
  240.1 69.6 %reduce-scatter.5.cloned.1.call-done = f32[64,8,128]{2,0,1:T(8,128)} async-done(((f32[512,8,128]{2,0,1:T(8,128)}), f32[64,8,128]{2,0,1:T(8,128)}) %reduce-scatter.5.cloned.1.call-update) | async-done | bytes 262160 | tf_op jit(solution)/shard_map/reduce_scatter | solution.py:82
  309.8 1.7 copy_bitcast_fusion
  311.6 39.4 %all-gather.2.cloned.1.call-done = bf16[512,1024]{1,0:T(8,128)(2,1)} async-done(((bf16[64,1024]{1,0:T(8,128)(2,1)}), bf16[512,1024]{1,0:T(8,128)(2,1)}) %all-gather.2.cloned.1.call-update) | async-done | bytes 1048592 | tf_op jit(solution)/shard_map/all_gather | solution.py:88
  351.0 2.9 fusion.35
  354.0 35.0 %all-reduce.7.cloned.1.call-done = f32[512,512]{1,0:T(8,128)} async-done(((f32[512,512]{1,0:T(8,128)}), f32[512,512]{1,0:T(8,128)}) %all-reduce.7.cloned.1.call-update) | async-done | bytes 1048592 | tf_op jit(solution)/shard_map/psum | solution.py:32
  389.0 1.4 multiply_reduce_fusion
  390.4 3.2 fusion.26
  393.7 22.3 %psum.46 = f32[512]{0:T(512)S(1)} all-reduce(f32[512]{0:T(512)S(1)} %get-tuple-element.84), channel_id=1, replica_groups=mesh['tok'=8,'head'=4] {'tok'}, use_global_device_ids=true, to_apply=%region_13.14 | all-reduce | flops 512 | bytes 4096 | tf_op jit(solution)/shard_map/psum | solution.py:26
  416.0 80.2 %all-reduce.9.cloned.1.call-done = f32[512,1024]{1,0:T(8,128)} async-done(((f32[512,1024]{1,0:T(8,128)}), f32[512,1024]{1,0:T(8,128)}) %all-reduce.9.cloned.1.call-update) | async-done | bytes 2097168 | tf_op jit(solution)/shard_map/psum | solution.py:26
  496.3 3.8 fusion.23
  500.1 36.0 %all-reduce.11.cloned.1.call-done = f32[512,512]{1,0:T(8,128)} async-done(((f32[512,512]{1,0:T(8,128)}), f32[512,512]{1,0:T(8,128)}) %all-reduce.11.cloned.1.call-update) | async-done | bytes 1048592 | tf_op jit(solution)/shard_map/psum | solution.py:32
  536.0 2.4 add.46
  (36 shorter events, 0.6 us)
Async XLA Ops:
  6.5 1.2 copy-start
  6.5 109.5 %all-reduce.5.cloned.1.call-start = ((), (), s32[]{:S(2)}) async-start(), calls=%async_computation.2 | async-start | bytes 4194304 | tf_op jit(solution)/shard_map/psum | solution.py:26
  11.0 1.0 copy-start.2
  11.0 2.1 copy-start.3
  11.0 3.7 copy-start.1
  11.1 27.9 %copy-start.5 = (s32[256]{0:T(256)S(1)}, s32[256]{0:T(256)}, u32[]{:S(2)}) copy-start(s32[256]{0:T(256)} %param.16) | copy-start | bytes 3076
  11.1 228.2 %reduce-scatter.7.cloned.1.call-start = ((), (), s32[]{:S(2)}) async-start(), calls=%async_computation.8 | async-start | bytes 294912
  180.3 129.5 %reduce-scatter.5.cloned.1.call-start = ((), (), s32[]{:S(2)}) async-start(), calls=%async_computation.3 | async-start | bytes 2359296 | tf_op jit(solution)/shard_map/reduce_scatter | solution.py:82
  183.8 167.2 %copy-start.6 = (bf16[1024,512]{1,0:T(8,128)(2,1)S(1)}, bf16[1024,512]{1,0:T(8,128)(2,1)}, u32[]{:S(2)}) copy-start(bf16[1024,512]{1,0:T(8,128)(2,1)} %param.19) | copy-start | bytes 3145732
  183.9 167.1 %all-gather.2.cloned.1.call-start = ((), (), s32[]{:S(2)}) async-start(), calls=%async_computation.4 | async-start | bytes 1179648 | tf_op jit(solution)/shard_map/all_gather | solution.py:88
  311.5 77.4 %all-reduce.7.cloned.1.call-start = ((), (), s32[]{:S(2)}) async-start(), calls=%async_computation.5 | async-start | bytes 2097152 | tf_op jit(solution)/shard_map/psum | solution.py:32
  353.9 36.5 %copy-start.4 = (f32[512]{0:T(512)S(1)}, f32[512]{0:T(512)}, u32[]{:S(2)}) copy-start(f32[512]{0:T(512)} %param.23) | copy-start | bytes 6148
  353.9 142.3 %all-reduce.9.cloned.1.call-start = ((), (), s32[]{:S(2)}) async-start(), calls=%async_computation.6 | async-start | bytes 4194304 | tf_op jit(solution)/shard_map/psum | solution.py:26
  393.6 142.4 %all-reduce.11.cloned.1.call-start = ((), (), s32[]{:S(2)}) async-start(), calls=%async_computation.7 | async-start | bytes 2097152 | tf_op jit(solution)/shard_map/psum | solution.py:32
Sparse Core Ops, SparseCore 0:
  11.2 104.8 all-reduce.4
  180.4 58.8 reduce-scatter.6
  242.8 66.8 reduce-scatter.4
  311.8 39.1 all-gather.1
  354.1 34.8 all-reduce.6
  393.8 102.4 all-reduce.8
  500.2 35.7 all-reduce.10
where the time goes:
time: 547 us; the launch traced here: 545 us
  waiting for transfers between devices  393 us (72%)
  blocking collectives  82.2 us (15%)
  matrix products  36.9 us (7%)
  between operations  14.2 us (3%)
  other arithmetic  11.9 us (2%)
  local copies, waits for them, and re-layouts  6.73 us (1%)
    psum x2, waiting for transfers between devices, projected(): squares, summed = lax.psum((squares, partial_rows), 'tok')  157 us
    psum x2, waiting for transfers between devices, head_update(): lax.psum(jnp.dot(full_rows, weight, preferred_element_type=jnp.float32),...  70.9 us
    reduce_scatter x1, waiting for transfers between devices, shards(): lax.psum_scatter(weighted * factor[:, :, None], 'tok', scatter_dimension=...  69.6 us
    unnamed x8, waiting for transfers between devices  55.5 us
    psum x2, blocking collectives, projected(): squares, summed = lax.psum((squares, partial_rows), 'tok')  46.4 us
    all_gather x1, waiting for transfers between devices, shards(): attended = lax.all_gather(attended_rows, 'tok', axis=0, tiled=True)  39.4 us
    pmax x1, blocking collectives, shards(): ceiling = lax.pmax(highest, 'tok')  35.8 us
    dot_general x8, matrix products, one_head(): jnp.dot(weights.astype(jnp.bfloat16), value_one, preferred_element_type=j...  14.7 us
  transfers between devices with their start and end apart: 7, of which 7 were waited for; matrix products, arithmetic and copies ran while one was open for 1% of the time, Pallas kernels for 0%

commit v1 on v0

v1 whole, which is shorter than its diff:
```python
import functools

import jax
import jax.numpy as jnp
from jax import lax
from jax.experimental import pallas as pl
from jax.experimental.pallas import tpu as pltpu
from jax.sharding import PartitionSpec as P

HS = 128
epsilon = 1e-05
masked_score = -1e30
MESH = pl.DeviceIdType.MESH
f32 = jnp.float32
bf16 = jnp.bfloat16
RS_TYPES = (f32, f32, bf16)
UNROLL = 8


def chunk_count(latent_count, nz):
    count = 1
    while (
        latent_count % (2 * count) == 0
        and latent_count // (2 * count) >= 128
        and latent_count // (2 * count) // nz >= 16
    ):
        count *= 2
    return count


def each(first, last, body):
    if last - first <= UNROLL:
        for d in range(first, last):
            body(d)
    else:

        @pl.loop(first, last)
        def _(d):
            body(d)


def kernel(
    n_tok, n_head, chunks, width,
    lat_ref, key_ref, val_ref, bias_ref, gain_ref, mgain_ref,
    qw_hbm, ow_hbm, uw_hbm, dw_hbm,
    out_ref,
    qw, ow, uw, dw, vt,
    s1_0, s1_1, s1_2, r1_0, r1_1, r1_2, a_0, a_1, a_2, s2_0, s2_1, s2_2, q2_0, q2_1, q2_2,
    g_0, g_1, g_2,
    sq_s, sq_r, st_s, st_r, wt, fac_ref, inv_ref,
    h1s, h1r, h2, state_ref,
    w_sem, c_send, c_recv, t_send, t_recv, h_send, h_recv,
):
    tok = lax.axis_index("tok")
    head = lax.axis_index("head")
    nz = n_tok // 2
    nq = n_head // 2
    z = tok // 2
    b = tok % 2
    hq = head // 2
    hb = head % 2
    rows = lat_ref.shape[0] // chunks
    rg = rows // nz
    hr = rows // 2
    ch = key_ref.shape[1] // 2
    heads = key_ref.shape[1] // HS
    hh_n = heads // 2
    dt = lat_ref.shape[1]
    s1, r1, acc, s2, q2, g = (
        (s1_0, s1_1, s1_2), (r1_0, r1_1, r1_2), (a_0, a_1, a_2), (s2_0, s2_1, s2_2),
        (q2_0, q2_1, q2_2), (g_0, g_1, g_2),
    )
    drains = []

    def zpeer(d):
        return lax.rem(z + d, nz)

    def zfrom(d):
        return lax.rem(z + nz - d, nz)

    def to_tok(src, dst, ss, rs, t):
        return pltpu.make_async_remote_copy(
            src_ref=src, dst_ref=dst, send_sem=ss, recv_sem=rs,
            device_id=(t, head), device_id_type=MESH,
        )

    def to_head(src, dst, ss, rs, h):
        return pltpu.make_async_remote_copy(
            src_ref=src, dst_ref=dst, send_sem=ss, recv_sem=rs,
            device_id=(tok, h), device_id_type=MESH,
        )

    pair = 2 * z + (1 - b)
    hpair = 2 * hq + (1 - hb)

    weights = [
        pltpu.make_async_copy(src, dst, w_sem.at[i])
        for i, (src, dst) in enumerate(((qw_hbm, qw), (ow_hbm, ow), (uw_hbm, uw), (dw_hbm, dw)))
    ]
    for w in weights:
        w.start()

    barrier = pltpu.get_barrier_semaphore()

    def greet(t, h):
        pl.semaphore_signal(barrier, inc=1, device_id=(t, h), device_id_type=MESH)

    each(1, n_tok, lambda d: greet(lax.rem(tok + d, n_tok), head))
    each(1, nq, lambda d: greet(tok, 2 * lax.rem(hq + d, nq) + hb))
    greet(tok, hpair)
    pl.semaphore_wait(barrier, n_tok - 1 + nq)

    def started(make, first, last):
        each(first, last, lambda d: make(d).start())
        drains.append(lambda: each(first, last, lambda d: make(d).wait_send()))

    def pair_send(k, c):
        return to_tok(s1[k].at[c], r1[k].at[c], c_send.at[k, c, 0, 0], c_recv.at[k, c, 0, 0], pair)

    def group_send(k, c, d):
        src = acc[k] if s2[k].shape[0] != chunks else s2[k]
        return to_tok(
            src.at[c, pl.ds(zpeer(d) * rg, rg), :], q2[k].at[c, d],
            c_send.at[k, c, 1, d], c_recv.at[k, c, 1, d], 2 * zpeer(d) + b,
        )

    def share_send(k, c, d):
        at = g[k].at[c, b, pl.ds(z * rg, rg), :]
        return to_tok(at, at, c_send.at[k, c, 2, d], c_recv.at[k, c, 2, d], 2 * zpeer(d) + b)

    def share_recv(k, c, d):
        at = g[k].at[c, b, pl.ds(zfrom(d) * rg, rg), :]
        return to_tok(at, at, c_send.at[k, c, 2, d], c_recv.at[k, c, 2, d], 2 * zpeer(d) + b)

    def cross_send(k, c, d):
        at = g[k].at[c, b, pl.ds(zfrom(d) * rg, rg), :]
        return to_tok(at, at, c_send.at[k, c, 3, d], c_recv.at[k, c, 3, d], pair)

    def cross_recv(k, c, d):
        at = g[k].at[c, 1 - b, pl.ds(zfrom(d) * rg, rg), :]
        return to_tok(at, at, c_send.at[k, c, 3, d], c_recv.at[k, c, 3, d], pair)

    def sum_pair(k, c):
        pair_send(k, c).wait_recv()
        total = acc[k][c] + r1[k][c].astype(f32)
        acc[k][c] = total
        if s2[k].shape[0] == chunks:
            s2[k][c] = total.astype(s2[k].dtype)
        started(functools.partial(group_send, k, c), 1, nz)

    def sum_groups(k, c, finish):
        each(1, nz, lambda d: group_send(k, c, d).wait_recv())
        total = acc[k][c, pl.ds(z * rg, rg), :]
        for d in range(1, nz):
            total = total + q2[k][c, d].astype(f32)
        g[k][c, b, pl.ds(z * rg, rg), :] = finish(total)
        started(functools.partial(share_send, k, c), 1, nz)
        started(functools.partial(cross_send, k, c), 0, 1)

    def forward(k, c):
        def one(d):
            share_recv(k, c, d).wait_recv()
            cross_send(k, c, d).start()

        each(1, nz, one)
        drains.append(lambda: each(1, nz, lambda d: cross_send(k, c, d).wait_send()))

    def gathered(k, c):
        each(0, nz, lambda d: cross_recv(k, c, d).wait_recv())

    def note_send(i, src, dst, c, d):
        return to_tok(
            src, dst.at[d], t_send.at[i, c, d], t_recv.at[i, c, d], lax.rem(tok + d, n_tok)
        )

    def squares_send(k, c, d):
        return note_send(k, sq_s.at[k, c], sq_r.at[k, c], c, d)

    def stats_send(c, d):
        return note_send(2, st_s.at[c], st_r.at[c], c, d)

    def project(k, n, c, state, gain, weight):
        squares = jnp.sum(state * state, axis=1, keepdims=True)
        sq_s[k, c] = jnp.broadcast_to(squares, (rows, 128)).T[0:8, :]
        started(functools.partial(squares_send, k, c), 1, n_tok)
        scaled = (state * gain).astype(bf16)
        tile = min(256, ch)
        for j in range(0, ch, tile):
            part = jnp.dot(
                scaled, weight[:, pl.ds((1 - b) * ch + j, tile)], preferred_element_type=f32
            )
            s1[n][c, :, j : j + tile] = part.astype(s1[n].dtype)
        started(lambda d: pair_send(n, c), 0, 1)
        for j in range(0, ch, tile):
            acc[n][c, :, j : j + tile] = jnp.dot(
                scaled, weight[:, pl.ds(b * ch + j, tile)], preferred_element_type=f32
            )

    def scale_rows(k, c, total):
        each(1, n_tok, lambda d: squares_send(k, c, d).wait_recv())
        squares = sq_s[k, c]
        for d in range(1, n_tok):
            squares = squares + sq_r[k, c, d]
        inverse = lax.rsqrt(squares / width + epsilon)
        inv_ref[...] = jnp.broadcast_to(inverse[0:1, :], (128, rows)).T
        mine = inv_ref[pl.ds(z * rg, rg), :]
        return total * jnp.concatenate([mine] * (ch // 128), axis=1)

    def attend(c):
        for hh in range(hh_n):
            for half in range(2):
                h = half * hh_n + hh
                query = g[0][c, half, :, hh * HS : (hh + 1) * HS]
                scores = lax.dot_general(
                    key_ref[:, h * HS : (h + 1) * HS], query, (((1,), (1,)), ((), ())),
                    preferred_element_type=f32,
                ) * HS ** (-0.5)
                scores = jnp.where(
                    jnp.concatenate([bias_ref[...]] * (rows // 128), axis=1) > 0.5,
                    scores, masked_score,
                )
                highest = jnp.max(scores, axis=0, keepdims=True)
                weights_b = jnp.exp(scores - highest)
                st_s[c, h : h + 1, :] = highest
                st_s[c, heads + h : heads + h + 1, :] = jnp.sum(weights_b, axis=0, keepdims=True)
                wt[c, h] = jnp.dot(
                    vt[h * HS : (h + 1) * HS, :], weights_b.astype(bf16), preferred_element_type=f32
                )
        started(functools.partial(stats_send, c), 1, n_tok)

    def normalise(c):
        each(1, n_tok, lambda d: stats_send(c, d).wait_recv())
        mine = st_s[c]
        top = mine[0:heads]
        for d in range(1, n_tok):
            top = jnp.maximum(top, st_r[c, d, 0:heads, :])
        own = jnp.exp(mine[0:heads] - top)
        den = own * mine[heads:]
        for d in range(1, n_tok):
            den = den + jnp.exp(st_r[c, d, 0:heads, :] - top) * st_r[c, d, heads : 2 * heads, :]
        fac_ref[...] = own / den
        for hh in range(hh_n):
            h = (1 - b) * hh_n + hh
            part = (wt[c, h] * fac_ref[pl.ds(h, 1), :]).T
            s1[1][c, :, hh * HS : (hh + 1) * HS] = part.astype(s1[1].dtype)
        started(lambda d: pair_send(1, c), 0, 1)
        for hh in range(hh_n):
            h = b * hh_n + hh
            acc[1][c, :, hh * HS : (hh + 1) * HS] = (wt[c, h] * fac_ref[pl.ds(h, 1), :]).T

    def hpair_send(m, c):
        return to_head(
            h1s.at[m, c, pl.ds((1 - hb) * hr, hr), :], h1r.at[m, c],
            h_send.at[m, c, 0, 0], h_recv.at[m, c, 0, 0], hpair,
        )

    def hdirect_send(m, c, d):
        at = h2.at[m, c, hq]
        return to_head(
            at, at, h_send.at[m, c, 1, d], h_recv.at[m, c, 1, d], 2 * lax.rem(hq + d, nq) + hb
        )

    def hdirect_recv(m, c, d):
        at = h2.at[m, c, lax.rem(hq + nq - d, nq)]
        return to_head(
            at, at, h_send.at[m, c, 1, d], h_recv.at[m, c, 1, d], 2 * lax.rem(hq + d, nq) + hb
        )

    def hback(m, c, half):
        at = (state_ref if m == 0 else out_ref).at[pl.ds(c * rows + half * hr, hr), :]
        return to_head(at, at, h_send.at[m, c, 2, 0], h_recv.at[m, c, 2, 0], hpair)

    def head_partial(m, c, k, weight):
        tile = min(256, dt)
        left, right = g[k][c, 0], g[k][c, 1]
        for j in range(0, dt, tile):
            h1s[m, c, :, j : j + tile] = jnp.dot(
                left, weight[0:ch, j : j + tile], preferred_element_type=f32
            ) + jnp.dot(right, weight[ch : 2 * ch, j : j + tile], preferred_element_type=f32)
        started(lambda d: hpair_send(m, c), 0, 1)

    def head_pair(m, c):
        hpair_send(m, c).wait_recv()
        h2[m, c, hq] = h1s[m, c, pl.ds(hb * hr, hr), :] + h1r[m, c]
        started(functools.partial(hdirect_send, m, c), 1, nq)

    def head_total(m, c):
        each(1, nq, lambda d: hdirect_recv(m, c, d).wait_recv())
        total = h2[m, c, 0]
        for i in range(1, nq):
            total = total + h2[m, c, i]
        at = pl.ds(c * rows + hb * hr, hr)
        if m == 0:
            state_ref[at, :] = lat_ref[at, :] + total
        else:
            out_ref[at, :] = state_ref[at, :] + total
        started(lambda d: hback(m, c, hb), 0, 1)

    def head_back(m, c):
        hback(m, c, 1 - hb).wait_recv()

    def stage_0(c):
        if c == 0:
            weights[0].wait()
        project(0, 0, c, lat_ref[c * rows : (c + 1) * rows, :], gain_ref[...], qw)
        if c == chunks - 1:
            for h in range(heads):
                vt[h * HS : (h + 1) * HS, :] = (
                    val_ref[:, h * HS : (h + 1) * HS].astype(f32).T.astype(bf16)
                )

    def stage_2(c):
        sum_groups(0, c, lambda t: scale_rows(0, c, t).astype(bf16))

    def stage_4(c):
        gathered(0, c)
        attend(c)

    def stage_9(c):
        if c == 0:
            weights[1].wait()
        gathered(1, c)
        head_partial(0, c, 1, ow)

    def stage_12(c):
        if c == 0:
            weights[2].wait()
        head_back(0, c)
        project(1, 2, c, state_ref[c * rows : (c + 1) * rows, :], mgain_ref[...], uw)

    def pair_2(c):
        sum_pair(2, c)

    def stage_14(c):
        sum_groups(2, c, lambda t: jax.nn.gelu(scale_rows(1, c, t)).astype(bf16))

    def stage_16(c):
        if c == 0:
            weights[3].wait()
        gathered(2, c)
        head_partial(1, c, 2, dw)

    stages = [
        stage_0,
        lambda c: sum_pair(0, c),
        stage_2,
        lambda c: forward(0, c),
        stage_4,
        normalise,
        lambda c: sum_pair(1, c),
        lambda c: sum_groups(1, c, lambda t: t.astype(bf16)),
        lambda c: forward(1, c),
        stage_9,
        lambda c: head_pair(0, c),
        lambda c: head_total(0, c),
        stage_12,
        pair_2,
        stage_14,
        lambda c: forward(2, c),
        stage_16,
        lambda c: head_pair(1, c),
        lambda c: head_total(1, c),
        lambda c: head_back(1, c),
    ]
    for step in range(len(stages) + chunks - 1):
        for c in range(chunks):
            if 0 <= step - c < len(stages):
                stages[step - c](c)
    for drain in drains:
        drain()


def shards(
    n_tok, n_head, latents, doc_keys, doc_values, token_mask, shard_lengths,
    query_weight, output_weight, attn_gain, up_weight, down_weight, mlp_gain,
):
    token_count, features = doc_keys.shape
    latent_count, dt = latents.shape
    positions = jnp.arange(token_count, dtype=jnp.int32)
    valid = (token_mask == 1) & (positions < shard_lengths[0])
    bias = jnp.broadcast_to(valid.astype(f32)[:, None], (token_count, 128))
    nz, nq = n_tok // 2, n_head // 2
    chunks = chunk_count(latent_count, nz)
    rows = latent_count // chunks
    rg, ch, heads = rows // nz, features // 2, features // HS

    def per(make):
        return [make(t) for t in RS_TYPES]

    scratch = [
        pltpu.VMEM(query_weight.shape, bf16), pltpu.VMEM(output_weight.shape, bf16),
        pltpu.VMEM(up_weight.shape, bf16), pltpu.VMEM(down_weight.shape, bf16),
        pltpu.VMEM((features, token_count), bf16),
        *per(lambda t: pltpu.VMEM((chunks, rows, ch), t)),
        *per(lambda t: pltpu.VMEM((chunks, rows, ch), t)),
        *per(lambda t: pltpu.VMEM((chunks, rows, ch), f32)),
        *per(lambda t: pltpu.VMEM((chunks, rows, ch) if t != f32 else (chunks + 1, 8, 128), t)),
        *per(lambda t: pltpu.VMEM((chunks, nz, rg, ch), t)),
        *per(lambda t: pltpu.VMEM((chunks, 2, rows, ch), bf16)),
        pltpu.VMEM((2, chunks, 8, rows), f32),
        pltpu.VMEM((2, chunks, n_tok, 8, rows), f32),
        pltpu.VMEM((chunks, 2 * heads, rows), f32),
        pltpu.VMEM((chunks, n_tok, 2 * heads, rows), f32),
        pltpu.VMEM((chunks, heads, HS, rows), f32),
        pltpu.VMEM((heads, rows), f32),
        pltpu.VMEM((rows, 128), f32),
        pltpu.VMEM((2, chunks, rows, dt), f32),
        pltpu.VMEM((2, chunks, rows // 2, dt), f32),
        pltpu.VMEM((2, chunks, nq, rows // 2, dt), f32),
        pltpu.VMEM((latent_count, dt), f32),
        pltpu.SemaphoreType.DMA((4,)),
        pltpu.SemaphoreType.DMA((3, chunks, 4, nz)),
        pltpu.SemaphoreType.DMA((3, chunks, 4, nz)),
        pltpu.SemaphoreType.DMA((3, chunks, n_tok)),
        pltpu.SemaphoreType.DMA((3, chunks, n_tok)),
        pltpu.SemaphoreType.DMA((2, chunks, 3, nq)),
        pltpu.SemaphoreType.DMA((2, chunks, 3, nq)),
    ]
    vmem = pl.BlockSpec(memory_space=pltpu.VMEM)
    anywhere = pl.BlockSpec(memory_space=pl.ANY)
    return pl.pallas_call(
        functools.partial(kernel, n_tok, n_head, chunks, dt * n_tok),
        out_shape=jax.ShapeDtypeStruct(latents.shape, f32),
        in_specs=[vmem] * 6 + [anywhere] * 4,
        out_specs=vmem,
        scratch_shapes=scratch,
        compiler_params=pltpu.CompilerParams(
            collective_id=0, has_side_effects=True, vmem_limit_bytes=56 * 1024 * 1024
        ),
    )(
        latents, doc_keys, doc_values, bias, attn_gain[None, :], mlp_gain[None, :],
        query_weight, output_weight, up_weight, down_weight,
    )


def solution(mesh):
    in_specs = (
        P(None, "tok"),
        P("tok", "head"),
        P("tok", "head"),
        P("tok"),
        P("tok"),
        P("tok", "head"),
        P("head", "tok"),
        P("tok"),
        P("tok", "head"),
        P("head", "tok"),
        P("tok"),
    )
    return jax.shard_map(
        functools.partial(shards, mesh.shape["tok"], mesh.shape["head"]),
        mesh=mesh, in_specs=in_specs, out_specs=P(None, "tok"), check_vma=False,
    )
```

time: 547 us -> 155 us (0.28)
  waiting for transfers between devices: 393 us -> 0 us
  Pallas kernels: 0 us -> 151 us
  blocking collectives: 82.2 us -> 0 us
  matrix products: 36.9 us -> 0 us
  between operations: 14.2 us -> 0.67 us
  other arithmetic: 11.9 us -> 0.01 us
    psum x4 -> x0, waiting for transfers between devices: 228 us -> none  [the longest x2 157 us: projected(): squares, summed = lax.psum((squares, partial_rows), 'tok')]
    pallas_call x0 -> x1, Pallas kernels: none -> 151 us  [shards(): pl.pallas_call(functools.partial(kernel, n_tok, n_head, chunks, dt * n_to...]
    reduce_scatter x1 -> x0, waiting for transfers between devices: 69.6 us -> none  [shards(): lax.psum_scatter(weighted * factor[:, :, None], 'tok', scatter_dimension=...]
    unnamed x8 -> x0, waiting for transfers between devices: 55.5 us -> none
    psum x2 -> x0, blocking collectives: 46.4 us -> none  [projected(): squares, summed = lax.psum((squares, partial_rows), 'tok')]
    all_gather x1 -> x0, waiting for transfers between devices: 39.4 us -> none  [shards(): attended = lax.all_gather(attended_rows, 'tok', axis=0, tiled=True)]
    dot_general x20 -> x0, matrix products: 36.9 us -> none  [the longest x8 14.7 us: one_head(): jnp.dot(weights.astype(jnp.bfloat16), value_one, preferred_element_type=j...]
    pmax x1 -> x0, blocking collectives: 35.8 us -> none  [shards(): ceiling = lax.pmax(highest, 'tok')]
  transfers between devices with their start and end apart: 7 -> 0, of which waited for: 7 -> 0; matrix products, arithmetic and copies ran while one was open for 1% -> 0% of each run, Pallas kernels for 0% -> 0%
where the time goes in v1:
time: 155 us
  Pallas kernels  151 us (97%)
  local copies, waits for them, and re-layouts  3.69 us (2%)
    pallas_call x1, Pallas kernels, shards(): pl.pallas_call(functools.partial(kernel, n_tok, n_head, chunks, dt * n_to...  151 us

profile of v1, /device:TPU:0, one launch (start us, length us, event | category | flops | bytes accessed | tf_op | source)
XLA Modules:
  0.0 154.9 jit_solution(14736556837227079193)
XLA Ops:
  0.7 0.0 copy-start
  0.7 0.7 copy-done
  1.3 0.8 broadcast_in_dim.12.bias_ref
  2.1 150.6 %shard_map.109 = f32[512,512]{1,0:T(8,128)} custom-call(f32[512,512]{1,0:T(8,128)} %lat_ref.1, bf16[256,1024]{1,0:T(8,128)(2,1)} %key_ref.1, bf16[256,1024]{1,0:T(8,128)(2,1)} %val_ref.1, f32[256,128]{1,0:T(8,128)} %broadcast_in_dim.12.bias_ref, f32[1,512]{1,0:T(1,128)} %bitcast.4, f32[1,512]{1,0:T(1,128)} %bitcast.5, bf16[512,1024]{1,0:T(8,128)(2,1)} %qw_hbm.1, ...), custom_call_target="tpu_custom_call" | custom-call | tf_op jit(solution)/shard_map/pallas_call | solution.py:421
  152.7 2.3 %copy.14 = f32[512,512]{1,0:T(8,128)} copy(f32[512,512]{1,0:T(8,128)} %shard_map.109) | data formatting | bytes 2097152
  (1 shorter events, 0.0 us)
Async XLA Ops:
  0.7 0.7 copy-start

commit v2 on v1

--- a/solution.py
+++ b/solution.py
@@ -13,7 +13,10 @@
 MESH = pl.DeviceIdType.MESH
 f32 = jnp.float32
 bf16 = jnp.bfloat16
-RS_TYPES = (f32, f32, bf16)
+RS_TYPES = (f32, jnp.int16, bf16)
+FULL = 32000.0
+KV_AT = 1
+SKEW = 1
 UNROLL = 8
 
 
@@ -47,9 +50,9 @@
     qw, ow, uw, dw, vt,
     s1_0, s1_1, s1_2, r1_0, r1_1, r1_2, a_0, a_1, a_2, s2_0, s2_1, s2_2, q2_0, q2_1, q2_2,
     g_0, g_1, g_2,
-    sq_s, sq_r, st_s, st_r, wt, fac_ref, inv_ref,
+    sq_s, sq_r, st_s, st_r, wt, inv_ref, k2, v2, bias2, mask, scale_ref,
     h1s, h1r, h2, state_ref,
-    w_sem, c_send, c_recv, t_send, t_recv, h_send, h_recv,
+    w_sem, c_send, c_recv, t_send, t_recv, h_send, h_recv, kv_send, kv_recv,
 ):
     tok = lax.axis_index("tok")
     head = lax.axis_index("head")
@@ -63,8 +66,8 @@
     rg = rows // nz
     hr = rows // 2
     ch = key_ref.shape[1] // 2
-    heads = key_ref.shape[1] // HS
-    hh_n = heads // 2
+    hh_n = ch // HS
+    token_count = key_ref.shape[0]
     dt = lat_ref.shape[1]
     s1, r1, acc, s2, q2, g = (
         (s1_0, s1_1, s1_2), (r1_0, r1_1, r1_2), (a_0, a_1, a_2), (s2_0, s2_1, s2_2),
@@ -152,10 +155,14 @@
         each(1, nz, lambda d: group_send(k, c, d).wait_recv())
         total = acc[k][c, pl.ds(z * rg, rg), :]
         for d in range(1, nz):
-            total = total + q2[k][c, d].astype(f32)
+            term = q2[k][c, d].astype(f32)
+            if k == 1:
+                term = term * jnp.concatenate([scale_ref[c, 1:2, :]] * hh_n, axis=1)
+            total = total + term
         g[k][c, b, pl.ds(z * rg, rg), :] = finish(total)
         started(functools.partial(share_send, k, c), 1, nz)
-        started(functools.partial(cross_send, k, c), 0, 1)
+        if k > 0:
+            started(functools.partial(cross_send, k, c), 0, 1)
 
     def forward(k, c):
         def one(d):
@@ -168,16 +175,14 @@
     def gathered(k, c):
         each(0, nz, lambda d: cross_recv(k, c, d).wait_recv())
 
-    def note_send(i, src, dst, c, d):
-        return to_tok(
-            src, dst.at[d], t_send.at[i, c, d], t_recv.at[i, c, d], lax.rem(tok + d, n_tok)
-        )
+    def note_send(i, src, dst, c, d, t):
+        return to_tok(src, dst.at[d], t_send.at[i, c, d], t_recv.at[i, c, d], t)
 
     def squares_send(k, c, d):
-        return note_send(k, sq_s.at[k, c], sq_r.at[k, c], c, d)
+        return note_send(k, sq_s.at[k, c], sq_r.at[k, c], c, d, lax.rem(tok + d, n_tok))
 
     def stats_send(c, d):
-        return note_send(2, st_s.at[c], st_r.at[c], c, d)
+        return note_send(2, st_s.at[c], st_r.at[c], c, d, 2 * zpeer(d) + b)
 
     def project(k, n, c, state, gain, weight):
         squares = jnp.sum(state * state, axis=1, keepdims=True)
@@ -206,47 +211,91 @@
         mine = inv_ref[pl.ds(z * rg, rg), :]
         return total * jnp.concatenate([mine] * (ch // 128), axis=1)
 
+    def doc_sends():
+        cols = pl.ds((1 - b) * ch, ch)
+        return [
+            to_tok(src, dst, kv_send.at[i], kv_recv.at[i], pair)
+            for i, (src, dst) in enumerate(
+                ((key_ref.at[:, cols], k2), (val_ref.at[:, cols], v2), (bias_ref, bias2))
+            )
+        ]
+
+    def send_docs():
+        for copy in doc_sends():
+            copy.start()
+        drains.append(lambda: [copy.wait_send() for copy in doc_sends()])
+
+    def receive_docs():
+        for copy in doc_sends():
+            copy.wait_recv()
+        biggest = jnp.zeros((1, 128), f32)
+        for i, bias in enumerate((bias_ref, bias2)):
+            mask[i] = jnp.broadcast_to(bias[0:1, :], (128, token_count)).T
+            for hh in range(hh_n):
+                if i == 0:
+                    piece = val_ref[:, pl.ds(b * ch + hh * HS, HS)]
+                else:
+                    piece = v2[:, hh * HS : (hh + 1) * HS]
+                piece = piece.astype(f32)
+                biggest = jnp.maximum(biggest, jnp.max(jnp.abs(piece), axis=0, keepdims=True))
+                vt[i, hh * HS : (hh + 1) * HS, :] = piece.T.astype(bf16)
+        biggest = jnp.broadcast_to(jnp.max(biggest, axis=1, keepdims=True), (8, rows))
+        for c in range(chunks):
+            st_s[c, 2 * hh_n : 2 * hh_n + 8, :] = biggest
+
     def attend(c):
         for hh in range(hh_n):
-            for half in range(2):
-                h = half * hh_n + hh
-                query = g[0][c, half, :, hh * HS : (hh + 1) * HS]
+            query = g[0][c, b, :, hh * HS : (hh + 1) * HS]
+            parts = []
+            for i in range(2):
+                if i == 0:
+                    keys = key_ref[:, pl.ds(b * ch + hh * HS, HS)]
+                else:
+                    keys = k2[:, hh * HS : (hh + 1) * HS]
                 scores = lax.dot_general(
-                    key_ref[:, h * HS : (h + 1) * HS], query, (((1,), (1,)), ((), ())),
-                    preferred_element_type=f32,
+                    keys, query, (((1,), (1,)), ((), ())), preferred_element_type=f32
                 ) * HS ** (-0.5)
                 scores = jnp.where(
-                    jnp.concatenate([bias_ref[...]] * (rows // 128), axis=1) > 0.5,
-                    scores, masked_score,
+                    jnp.concatenate([mask[i]] * (rows // 128), axis=1) > 0.5, scores, masked_score
                 )
                 highest = jnp.max(scores, axis=0, keepdims=True)
                 weights_b = jnp.exp(scores - highest)
-                st_s[c, h : h + 1, :] = highest
-                st_s[c, heads + h : heads + h + 1, :] = jnp.sum(weights_b, axis=0, keepdims=True)
-                wt[c, h] = jnp.dot(
-                    vt[h * HS : (h + 1) * HS, :], weights_b.astype(bf16), preferred_element_type=f32
+                total = jnp.sum(weights_b, axis=0, keepdims=True)
+                weighted = jnp.dot(
+                    vt[i, hh * HS : (hh + 1) * HS, :], weights_b.astype(bf16),
+                    preferred_element_type=f32,
                 )
-        started(functools.partial(stats_send, c), 1, n_tok)
+                parts.append((highest, total, weighted))
+            (top_0, total_0, sum_0), (top_1, total_1, sum_1) = parts
+            top = jnp.maximum(top_0, top_1)
+            left, right = jnp.exp(top_0 - top), jnp.exp(top_1 - top)
+            st_s[c, hh : hh + 1, :] = top
+            st_s[c, hh_n + hh : hh_n + hh + 1, :] = left * total_0 + right * total_1
+            wt[c, hh] = sum_0 * left + sum_1 * right
+        started(functools.partial(stats_send, c), 1, nz)
 
     def normalise(c):
-        each(1, n_tok, lambda d: stats_send(c, d).wait_recv())
+        each(1, nz, lambda d: stats_send(c, d).wait_recv())
         mine = st_s[c]
-        top = mine[0:heads]
-        for d in range(1, n_tok):
-            top = jnp.maximum(top, st_r[c, d, 0:heads, :])
-        own = jnp.exp(mine[0:heads] - top)
-        den = own * mine[heads:]
-        for d in range(1, n_tok):
-            den = den + jnp.exp(st_r[c, d, 0:heads, :] - top) * st_r[c, d, heads : 2 * heads, :]
-        fac_ref[...] = own / den
+        top, biggest = mine[0:hh_n], mine[2 * hh_n :]
+        for d in range(1, nz):
+            top = jnp.maximum(top, st_r[c, d, 0:hh_n, :])
+            biggest = jnp.maximum(biggest, st_r[c, d, 2 * hh_n :, :])
+        own = jnp.exp(mine[0:hh_n] - top)
+        den = own * mine[hh_n : 2 * hh_n]
+        for d in range(1, nz):
+            den = den + jnp.exp(st_r[c, d, 0:hh_n, :] - top) * st_r[c, d, hh_n : 2 * hh_n, :]
+        factor = own / den
+        biggest = jnp.maximum(biggest[0:1, 0:128], 1e-30)
+        scale_ref[c, 0:1, :] = FULL / biggest
+        scale_ref[c, 1:2, :] = biggest / FULL
         for hh in range(hh_n):
-            h = (1 - b) * hh_n + hh
-            part = (wt[c, h] * fac_ref[pl.ds(h, 1), :]).T
-            s1[1][c, :, hh * HS : (hh + 1) * HS] = part.astype(s1[1].dtype)
-        started(lambda d: pair_send(1, c), 0, 1)
-        for hh in range(hh_n):
-            h = b * hh_n + hh
-            acc[1][c, :, hh * HS : (hh + 1) * HS] = (wt[c, h] * fac_ref[pl.ds(h, 1), :]).T
+            part = (wt[c, hh] * factor[hh : hh + 1, :]).T
+            acc[1][c, :, hh * HS : (hh + 1) * HS] = part
+            s2[1][c, :, hh * HS : (hh + 1) * HS] = (
+                jnp.round(part * scale_ref[c, 0:1, :]).astype(jnp.int32).astype(jnp.int16)
+            )
+        started(functools.partial(group_send, 1, c), 1, nz)
 
     def hpair_send(m, c):
         return to_head(
@@ -303,17 +352,16 @@
         if c == 0:
             weights[0].wait()
         project(0, 0, c, lat_ref[c * rows : (c + 1) * rows, :], gain_ref[...], qw)
-        if c == chunks - 1:
-            for h in range(heads):
-                vt[h * HS : (h + 1) * HS, :] = (
-                    val_ref[:, h * HS : (h + 1) * HS].astype(f32).T.astype(bf16)
-                )
+        if c == min(KV_AT, chunks - 1):
+            send_docs()
 
     def stage_2(c):
         sum_groups(0, c, lambda t: scale_rows(0, c, t).astype(bf16))
 
     def stage_4(c):
-        gathered(0, c)
+        if c == 0:
+            receive_docs()
+        each(1, nz, lambda d: share_recv(0, c, d).wait_recv())
         attend(c)
 
     def stage_9(c):
@@ -344,10 +392,8 @@
         stage_0,
         lambda c: sum_pair(0, c),
         stage_2,
-        lambda c: forward(0, c),
         stage_4,
         normalise,
-        lambda c: sum_pair(1, c),
         lambda c: sum_groups(1, c, lambda t: t.astype(bf16)),
         lambda c: forward(1, c),
         stage_9,
@@ -362,10 +408,10 @@
         lambda c: head_total(1, c),
         lambda c: head_back(1, c),
     ]
-    for step in range(len(stages) + chunks - 1):
+    for step in range(len(stages) + SKEW * (chunks - 1)):
         for c in range(chunks):
-            if 0 <= step - c < len(stages):
-                stages[step - c](c)
+            if 0 <= step - SKEW * c < len(stages):
+                stages[step - SKEW * c](c)
     for drain in drains:
         drain()
 
@@ -378,11 +424,11 @@
     latent_count, dt = latents.shape
     positions = jnp.arange(token_count, dtype=jnp.int32)
     valid = (token_mask == 1) & (positions < shard_lengths[0])
-    bias = jnp.broadcast_to(valid.astype(f32)[:, None], (token_count, 128))
+    bias = jnp.broadcast_to(valid.astype(f32)[None, :], (8, token_count))
     nz, nq = n_tok // 2, n_head // 2
     chunks = chunk_count(latent_count, nz)
     rows = latent_count // chunks
-    rg, ch, heads = rows // nz, features // 2, features // HS
+    rg, ch, hh_n = rows // nz, features // 2, features // (2 * HS)
 
     def per(make):
         return [make(t) for t in RS_TYPES]
@@ -390,7 +436,7 @@
     scratch = [
         pltpu.VMEM(query_weight.shape, bf16), pltpu.VMEM(output_weight.shape, bf16),
         pltpu.VMEM(up_weight.shape, bf16), pltpu.VMEM(down_weight.shape, bf16),
-        pltpu.VMEM((features, token_count), bf16),
+        pltpu.VMEM((2, ch, token_count), bf16),
         *per(lambda t: pltpu.VMEM((chunks, rows, ch), t)),
         *per(lambda t: pltpu.VMEM((chunks, rows, ch), t)),
         *per(lambda t: pltpu.VMEM((chunks, rows, ch), f32)),
@@ -399,11 +445,15 @@
         *per(lambda t: pltpu.VMEM((chunks, 2, rows, ch), bf16)),
         pltpu.VMEM((2, chunks, 8, rows), f32),
         pltpu.VMEM((2, chunks, n_tok, 8, rows), f32),
-        pltpu.VMEM((chunks, 2 * heads, rows), f32),
-        pltpu.VMEM((chunks, n_tok, 2 * heads, rows), f32),
-        pltpu.VMEM((chunks, heads, HS, rows), f32),
-        pltpu.VMEM((heads, rows), f32),
+        pltpu.VMEM((chunks, 2 * hh_n + 8, rows), f32),
+        pltpu.VMEM((chunks, nz, 2 * hh_n + 8, rows), f32),
+        pltpu.VMEM((chunks, hh_n, HS, rows), f32),
         pltpu.VMEM((rows, 128), f32),
+        pltpu.VMEM((token_count, ch), bf16),
+        pltpu.VMEM((token_count, ch), bf16),
+        pltpu.VMEM((8, token_count), f32),
+        pltpu.VMEM((2, token_count, 128), f32),
+        pltpu.VMEM((chunks, 8, 128), f32),
         pltpu.VMEM((2, chunks, rows, dt), f32),
         pltpu.VMEM((2, chunks, rows // 2, dt), f32),
         pltpu.VMEM((2, chunks, nq, rows // 2, dt), f32),
@@ -415,6 +465,8 @@
         pltpu.SemaphoreType.DMA((3, chunks, n_tok)),
         pltpu.SemaphoreType.DMA((2, chunks, 3, nq)),
         pltpu.SemaphoreType.DMA((2, chunks, 3, nq)),
+        pltpu.SemaphoreType.DMA((3,)),
+        pltpu.SemaphoreType.DMA((3,)),
     ]
     vmem = pl.BlockSpec(memory_space=pltpu.VMEM)
     anywhere = pl.BlockSpec(memory_space=pl.ANY)

time: 155 us -> 146 us (0.942)
  Pallas kernels: 151 us -> 141 us
    pallas_call x1, Pallas kernels: 151 us -> 141 us  [shards(): pl.pallas_call(functools.partial(kernel, n_tok, n_head, chunks, dt * n_to...]
where the time goes in v2:
time: 146 us
  Pallas kernels  141 us (97%)
  local copies, waits for them, and re-layouts  3.54 us (2%)
    pallas_call x1, Pallas kernels, shards(): pl.pallas_call(functools.partial(kernel, n_tok, n_head, chunks, dt * n_to...  141 us
    unnamed x3, local copies, waits for them, and re-layouts  2.94 us

profile of v2, /device:TPU:0, one launch (start us, length us, event | category | flops | bytes accessed | tf_op | source)
XLA Modules:
  0.0 145.7 jit_solution(3234256899088991987)
XLA Ops:
  0.7 0.0 copy-start
  0.7 0.7 copy-done
  1.3 0.6 broadcast_in_dim.12.bias_ref
  1.9 141.4 %shard_map.109 = f32[512,512]{1,0:T(8,128)} custom-call(f32[512,512]{1,0:T(8,128)} %lat_ref.1, bf16[256,1024]{1,0:T(8,128)(2,1)} %key_ref.1, bf16[256,1024]{1,0:T(8,128)(2,1)} %val_ref.1, f32[8,256]{1,0:T(8,128)} %broadcast_in_dim.12.bias_ref, f32[1,512]{1,0:T(1,128)} %bitcast.4, f32[1,512]{1,0:T(1,128)} %bitcast.5, bf16[512,1024]{1,0:T(8,128)(2,1)} %qw_hbm.1, ...), custom_call_target="tpu_custom_call" | custom-call | tf_op jit(solution)/shard_map/pallas_call | solution.py:473
  143.4 2.3 %copy.14 = f32[512,512]{1,0:T(8,128)} copy(f32[512,512]{1,0:T(8,128)} %shard_map.109) | data formatting | bytes 2097152
  (1 shorter events, 0.0 us)
Async XLA Ops:
  0.7 0.7 copy-start

commit v3 on v2

--- a/solution.py
+++ b/solution.py
@@ -15,8 +15,7 @@
 bf16 = jnp.bfloat16
 RS_TYPES = (f32, jnp.int16, bf16)
 FULL = 32000.0
-KV_AT = 1
-SKEW = 1
+
 UNROLL = 8
 
 
@@ -350,10 +349,9 @@
 
     def stage_0(c):
         if c == 0:
+            send_docs()
             weights[0].wait()
         project(0, 0, c, lat_ref[c * rows : (c + 1) * rows, :], gain_ref[...], qw)
-        if c == min(KV_AT, chunks - 1):
-            send_docs()
 
     def stage_2(c):
         sum_groups(0, c, lambda t: scale_rows(0, c, t).astype(bf16))
@@ -408,10 +406,12 @@
         lambda c: head_total(1, c),
         lambda c: head_back(1, c),
     ]
-    for step in range(len(stages) + SKEW * (chunks - 1)):
+    for c in range(chunks):
+        stages[0](c)
+    for step in range(1, len(stages) + chunks - 1):
         for c in range(chunks):
-            if 0 <= step - SKEW * c < len(stages):
-                stages[step - SKEW * c](c)
+            if 1 <= step - c < len(stages):
+                stages[step - c](c)
     for drain in drains:
         drain()
 

time: 146 us -> 152 us (1.041)
  Pallas kernels: 141 us -> 147 us
    pallas_call x1, Pallas kernels: 141 us -> 147 us  [shards(): pl.pallas_call(functools.partial(kernel, n_tok, n_head, chunks, dt * n_to...]
where the time goes in v3:
time: 152 us; the launch traced here: 151 us
  Pallas kernels  147 us (97%)
  local copies, waits for them, and re-layouts  3.54 us (2%)
    pallas_call x1, Pallas kernels, shards(): pl.pallas_call(functools.partial(kernel, n_tok, n_head, chunks, dt * n_to...  147 us

profile of v3, /device:TPU:0, one launch (start us, length us, event | category | flops | bytes accessed | tf_op | source)
XLA Modules:
  0.0 151.5 jit_solution(12768243840498778924)
XLA Ops:
  0.7 0.0 copy-start
  0.7 0.7 copy-done
  1.3 0.6 broadcast_in_dim.12.bias_ref
  1.9 147.3 %shard_map.109 = f32[512,512]{1,0:T(8,128)} custom-call(f32[512,512]{1,0:T(8,128)} %lat_ref.1, bf16[256,1024]{1,0:T(8,128)(2,1)} %key_ref.1, bf16[256,1024]{1,0:T(8,128)(2,1)} %val_ref.1, f32[8,256]{1,0:T(8,128)} %broadcast_in_dim.12.bias_ref, f32[1,512]{1,0:T(1,128)} %bitcast.4, f32[1,512]{1,0:T(1,128)} %bitcast.5, bf16[512,1024]{1,0:T(8,128)(2,1)} %qw_hbm.1, ...), custom_call_target="tpu_custom_call" | custom-call | tf_op jit(solution)/shard_map/pallas_call | solution.py:473
  149.2 2.3 %copy.14 = f32[512,512]{1,0:T(8,128)} copy(f32[512,512]{1,0:T(8,128)} %shard_map.109) | data formatting | bytes 2097152
  (1 shorter events, 0.0 us)
Async XLA Ops:
  0.7 0.7 copy-start
